TPU v7x, 32 devices: a whole 2x2x4 slice. The times are simulated.
32 devices in a mesh: groups: 2 (over y), tile: 4 (over x, core), cuts: 4 (over z).
Axes of the slice: x: 2, y: 2, z: 4, core: 2. Of those that a mesh axis runs over, the one named last changes fastest.
Arguments:
- trade: bfloat16 [16, 4, 256, 8192], P(('groups', 'cuts'), 'tile'), parts along dimension 0, may hold values from -6 to 6
- factor: bfloat16 [32768, 256], P(('groups', 'tile', 'cuts')), parts along dimension 0, may hold values from -0.375 to 0.375
- scales: float32 [16, 256], P(('groups', 'cuts')), parts along dimension 0, may hold values from 0.1 to 1.9
- core: float32 [512, 256], P('groups'), parts along dimension 0, may hold values from -4 to 4
Outputs:
- grad_factor: float32 [32768, 256], P(('groups', 'tile', 'cuts')), parts along dimension 0
- grad_window: float32 [1024, 256], P(('groups', 'cuts')), parts along dimension 0
- grad_core: float32 [512, 256], P('groups'), parts along dimension 0
- grad_scales: float32 [16, 256], P(('groups', 'cuts')), parts along dimension 0
There are 2 independent parts, one for each index of `groups`. A program takes and returns all parts, laid end to end along the dimension named above; each array names one. Nothing has to cross between parts.
All inputs are finite; a program needn't handle non-finite values.
Results may differ from a plain program's by a relative error of at most 0.00055.
Values may be sent and summed in bfloat16 or wider, within the bound.
A program may use at most 128 MiB of HBM per device.

v0:
```python
import math
import jax
import jax.numpy as jnp
from jax import lax
from jax.sharding import PartitionSpec as P

P_SIZE = 256


def swapped(value, axis, distance):
    mask = 2**distance
    pairs = [(source, source ^ mask) for source in range(lax.axis_size(axis))]
    return lax.ppermute(value, axis, pairs)


def from_root(block, axis, source):
    block = jnp.where(lax.axis_index(axis) == source, block, jnp.zeros_like(block))
    return lax.psum(block, axis)


def body(trade, factor, scales, core):
    n_cuts = lax.axis_size("cuts")
    band_index = lax.axis_index("tile") % 2
    months = trade.shape[0]
    rows_band = trade.shape[2]
    window_size = 2 * rows_band
    highest = lax.Precision.HIGHEST
    own_block = lax.all_gather(factor, "cuts", axis=0, tiled=True)
    block = own_block.shape[0]
    partner_block = swapped(own_block, "tile", 0)
    first_block = jnp.where(band_index == 0, own_block, partner_block)
    second_block = jnp.where(band_index == 0, partner_block, own_block)
    column_factor = jnp.concatenate([first_block, second_block], 0)
    window_block = from_root(own_block, "tile", 0)
    window_rows = lax.dynamic_slice_in_dim(window_block, band_index * rows_band, rows_band, 0)
    window32 = window_rows.astype(jnp.float32)
    coef = 1.0 / math.sqrt(months * n_cuts * window_size)
    acc_columns = jnp.zeros((2 * block, P_SIZE), jnp.float32)
    acc_window = jnp.zeros((rows_band, P_SIZE), jnp.float32)
    acc_core = jnp.zeros((P_SIZE, P_SIZE), jnp.float32)
    diag_terms = []
    for month in range(months):
        diag_k = scales[month]
        inner = diag_k[:, None] * core * diag_k[None, :]
        mapped = jnp.dot(window32, inner, precision=highest).astype(jnp.bfloat16)
        model = lax.dot_general(
            mapped, column_factor, (((1,), (1,)), ((), ())), preferred_element_type=jnp.float32
        )
        residual = (trade[month, 0].astype(jnp.float32) - model).astype(jnp.bfloat16)
        acc_columns = acc_columns + lax.dot_general(
            residual, mapped, (((0,), (0,)), ((), ())), preferred_element_type=jnp.float32
        )
        projected = jnp.dot(residual, column_factor, preferred_element_type=jnp.float32)
        acc_window = acc_window + jnp.dot(projected, inner.T, precision=highest)
        gram = jnp.dot(window32.T, projected, precision=highest)
        acc_core = acc_core + diag_k[:, None] * gram * diag_k[None, :]
        weighted = gram * core
        diag_terms.append(
            jnp.dot(weighted, diag_k, precision=highest)
            + jnp.dot(weighted.T, diag_k, precision=highest)
        )
    diag_stack = jnp.stack(diag_terms, 0)
    halves = acc_columns.reshape(2, block, P_SIZE)
    mine = jnp.where(band_index == 0, halves[0], halves[1])
    other = jnp.where(band_index == 0, halves[1], halves[0])
    received = swapped(other, "tile", 0)
    grad_factor = lax.psum_scatter(mine + received, "cuts", scatter_dimension=0, tiled=True)
    padded = lax.dynamic_update_slice_in_dim(
        jnp.zeros((window_size, P_SIZE), jnp.float32), acc_window, band_index * rows_band, 0
    )
    window_part = lax.psum_scatter(padded, "cuts", scatter_dimension=0, tiled=True)
    window_total = lax.psum(window_part, "tile")
    core_total = lax.psum(acc_core, ("tile", "cuts"))
    diag_total = lax.psum(diag_stack, "tile")
    return (-coef * grad_factor, -coef * window_total, -coef * core_total, -coef * diag_total)


def solution(mesh):
    return jax.shard_map(
        body,
        mesh=mesh,
        in_specs=(
            P(("groups", "cuts"), "tile", None, None),
            P(("groups", "tile", "cuts"), None),
            P(("groups", "cuts"), None),
            P("groups", None),
        ),
        out_specs=(
            P(("groups", "tile", "cuts"), None),
            P(("groups", "cuts"), None),
            P("groups", None),
            P(("groups", "cuts"), None),
        ),
        check_vma=False,
    )
```

profile of v0, /device:TPU:0, one launch (start us, length us, event | category | flops | bytes accessed | tf_op | source)
XLA Modules:
  0.0 385.2 jit_solution(4281532647967686441)
XLA Ops:
  7.2 0.0 all-gather.2.cloned.1.call-start
  7.2 0.7 all-gather.2.cloned.1.call-update
  7.9 0.0 all-reduce.4.cloned.1.call-start
  7.9 50.3 %all-gather.2.cloned.1.call-done = bf16[4096,256]{1,0:T(8,128)(2,1)} async-done(((bf16[1024,256]{1,0:T(8,128)(2,1)}), bf16[4096,256]{1,0:T(8,128)(2,1)}) %all-gather.2.cloned.1.call-update) | async-done | bytes 2097168 | tf_op jit(solution)/shard_map/all_gather | solution.py:28
  58.2 0.0 collective-permute-start
  58.2 4.5 %collective-permute-done = bf16[4096,256]{1,0:T(8,128)(2,1)} collective-permute-done((bf16[4096,256]{1,0:T(8,128)(2,1)}, bf16[4096,256]{1,0:T(8,128)(2,1)}, u32[]{:S(2)}, u32[]{:S(2)}) %collective-permute-start) | collective-permute-done | bytes 2097184 | tf_op jit(solution)/shard_map/ppermute | solution.py:13
  62.7 4.6 %broadcast_select_fusion.2 = (bf16[4096,256]{1,0:T(8,128)(2,1)S(1)}, bf16[4096,256]{1,0:T(8,128)(2,1)}, bf16[4096,256]{1,0:T(8,128)(2,1)}) fusion(bf16[4096,256]{1,0:T(8,128)(2,1)} %all-gather.2.cloned.1.call-done, bf16[4096,256]{1,0:T(8,128)(2,1)} %collective-permute-done, pred[]{:T(512)S(6)} %eq.6, pred[]{:T(512)S(6)} %eq.12), kind=kLoop, calls=%fused_computation.10 | loop fusion | flops 3145728 | bytes 10485762 | tf_op jit(solution)/shard_map/jit(_where)/select_n | solution.py:31
  67.4 0.0 all-reduce.4.cloned.1.call-update
  67.4 0.0 reduce-scatter.5.cloned.1.call-start
  67.5 50.2 %all-reduce.4.cloned.1.call-done = bf16[4096,256]{1,0:T(8,128)(2,1)} async-done(((bf16[4096,256]{1,0:T(8,128)(2,1)}), bf16[4096,256]{1,0:T(8,128)(2,1)}) %all-reduce.4.cloned.1.call-update) | async-done | bytes 2097168 | tf_op jit(solution)/shard_map/psum | solution.py:18
  117.6 1.3 convolution_convert_fusion.1
  119.0 4.3 %fusion = bf16[256,8192]{1,0:T(8,128)(2,1)S(1)} fusion(bf16[256,256]{1,0:T(8,128)(2,1)S(1)} %convolution_convert_fusion.1, bf16[2,1,256,8192]{3,2,1,0:T(8,128)(2,1)} %param.4, bf16[4096,256]{1,0:T(8,128)(2,1)} %get-tuple-element.5, bf16[4096,256]{1,0:T(8,128)(2,1)S(1)} %get-tuple-element.4), kind=kOutput, calls=%fused_computation.3 | convolution fusion | flops 1088421888 | bytes 12713984 | tf_op jit(solution)/shard_map/dot_general | solution.py:46
  123.2 1.5 convolution_convert_fusion
  124.7 9.6 %fusion.1 = bf16[256,8192]{1,0:T(8,128)(2,1)S(1)} fusion(bf16[256,256]{1,0:T(8,128)(2,1)S(1)} %convolution_convert_fusion, bf16[2,1,256,8192]{3,2,1,0:T(8,128)(2,1)} %param.4, bf16[4096,256]{1,0:T(8,128)(2,1)S(1)} %copy-done.6, bf16[4096,256]{1,0:T(8,128)(2,1)S(1)} %get-tuple-element.4), kind=kOutput, calls=%fused_computation.4 | convolution fusion | flops 1088421888 | bytes 12713984 | tf_op jit(solution)/shard_map/dot_general | solution.py:46
  134.4 1.3 fusion.43
  135.7 0.6 copy-done.2
  136.3 1.3 convolution_add_fusion
  137.7 2.8 slice_select_fusion
  140.5 1.6 copy-done
  142.2 4.2 %fusion.41 = f32[256,256]{1,0:T(8,128)S(1)} fusion(bf16[256,8192]{1,0:T(8,128)(2,1)} %copy-done.4, bf16[4096,256]{1,0:T(8,128)(2,1)} %get-tuple-element.5, bf16[4096,256]{1,0:T(8,128)(2,1)S(1)} %get-tuple-element.4), kind=kOutput, calls=%fused_computation.61 | convolution fusion | flops 1082130432 | bytes 8650752 | tf_op jit(solution)/shard_map/dot_general | solution.py:53
  146.4 0.5 fusion.7
  146.9 1.2 fusion.40
  148.2 0.5 fusion.2
  148.7 0.0 copy-start.5
  148.7 0.8 copy-done.5
  149.5 0.0 reduce-scatter.5.cloned.1.call-update
  149.5 0.0 all-reduce.8.cloned.1.call-start
  149.6 1.2 fusion.24
  150.8 1.9 multiply_add_fusion
  152.8 0.0 all-reduce.8.cloned.1.call-update
  152.8 0.0 all-reduce.6.cloned.1.call-start
  152.8 18.8 %reduce-scatter.5.cloned.1.call-done = f32[128,256]{1,0:T(8,128)} async-done(((f32[512,256]{1,0:T(8,128)}), f32[128,256]{1,0:T(8,128)}) %reduce-scatter.5.cloned.1.call-update) | async-done | bytes 131088 | tf_op jit(solution)/shard_map/reduce_scatter | solution.py:71
  171.6 0.0 all-reduce.6.cloned.1.call-update
  171.6 0.0 reduce-scatter.3.cloned.1.call-start
  171.7 7.4 %select_add_fusion = f32[4096,256]{1,0:T(8,128)} fusion(f32[4096,256]{1,0:T(8,128)} %collective-permute-done.1, f32[8192,256]{1,0:T(8,128)} %copy-done, pred[]{:T(512)S(6)} %eq.6), kind=kLoop, calls=%fused_computation.6 | loop fusion | flops 2097152 | bytes 16777216 | tf_op jit(solution)/shard_map/add | solution.py:67
  179.1 0.0 reduce-scatter.3.cloned.1.call-update
  179.1 0.3 fusion.20
  179.4 0.3 fusion.5
  179.6 0.3 fusion.17
  179.9 0.3 fusion.3
  180.3 5.7 %psum.31 = f32[2,256]{1,0:T(2,128)S(1)} all-reduce(f32[2,256]{1,0:T(2,128)S(1)} %pad_maximum_fusion.1), channel_id=1, replica_groups=mesh['groups'=2,'tile'=4,'cuts'=4] {'tile'}, use_global_device_ids=true, to_apply=%region_5.6 | all-reduce | flops 512 | bytes 4096 | tf_op jit(solution)/shard_map/psum | solution.py:74
  185.9 0.6 broadcast_multiply_fusion.3
  186.5 76.4 %all-reduce.8.cloned.1.call-done = f32[256,256]{1,0:T(8,128)} async-done(((f32[256,256]{1,0:T(8,128)}), f32[256,256]{1,0:T(8,128)}) %all-reduce.8.cloned.1.call-update) | async-done | bytes 262160 | tf_op jit(solution)/shard_map/psum | solution.py:73
  262.9 1.7 broadcast_multiply_fusion.1
  264.6 32.5 %all-reduce.6.cloned.1.call-done = f32[128,256]{1,0:T(8,128)} async-done(((f32[128,256]{1,0:T(8,128)}), f32[128,256]{1,0:T(8,128)}) %all-reduce.6.cloned.1.call-update) | async-done | bytes 131088 | tf_op jit(solution)/shard_map/psum | solution.py:72
  297.1 1.6 broadcast_multiply_fusion.2
  298.7 77.4 %reduce-scatter.3.cloned.1.call-done = f32[1024,256]{1,0:T(8,128)} async-done(((f32[4096,256]{1,0:T(8,128)}), f32[1024,256]{1,0:T(8,128)}) %reduce-scatter.3.cloned.1.call-update) | async-done | bytes 1048592 | tf_op jit(solution)/shard_map/reduce_scatter | solution.py:67
  376.1 2.3 broadcast_multiply_fusion
  (21 shorter events, 0.1 us)
Async XLA Ops:
  7.2 51.1 %all-gather.2.cloned.1.call-start = ((), (), s32[]{:S(2)}) async-start(), calls=%async_computation.2 | async-start | bytes 2621440 | tf_op jit(solution)/shard_map/all_gather | solution.py:28
  7.9 109.7 %all-reduce.4.cloned.1.call-start = ((), (), s32[]{:S(2)}) async-start(), calls=%async_computation.3 | async-start | bytes 4194304 | tf_op jit(solution)/shard_map/psum | solution.py:18
  58.2 4.5 %collective-permute-start = (bf16[4096,256]{1,0:T(8,128)(2,1)}, bf16[4096,256]{1,0:T(8,128)(2,1)}, u32[]{:S(2)}, u32[]{:S(2)}) collective-permute-start(bf16[4096,256]{1,0:T(8,128)(2,1)} %all-gather.2.cloned.1.call-done), channel_id=1, source_target_pairs={{0,4},{4,0},{8,12},{12,8},{1,5},{5,1},{9,13},{13,9},{2,6},{6,2},{1... | collective-permute-start | bytes 6291464 | tf_op jit(solution)/shard_map/ppermute | solution.py:13
  58.2 9.2 %copy-start.8 = (f32[2,256]{1,0:T(2,128)S(1)}, f32[2,256]{1,0:T(2,128)}, u32[]{:S(2)}) copy-start(f32[2,256]{1,0:T(2,128)} %param.6) | copy-start | bytes 6148
  58.2 59.4 %copy-start.1 = (f32[256,256]{1,0:T(8,128)S(1)}, f32[256,256]{1,0:T(8,128)}, u32[]{:S(2)}) copy-start(f32[256,256]{1,0:T(8,128)} %param.7) | copy-start | bytes 786436
  67.4 104.2 %reduce-scatter.5.cloned.1.call-start = ((), (), s32[]{:S(2)}) async-start(), calls=%async_computation.5 | async-start | bytes 655360 | tf_op jit(solution)/shard_map/reduce_scatter | solution.py:71
  118.9 5.8 %copy-start.6 = (bf16[4096,256]{1,0:T(8,128)(2,1)S(1)}, bf16[4096,256]{1,0:T(8,128)(2,1)}, u32[]{:S(2)}) copy-start(bf16[4096,256]{1,0:T(8,128)(2,1)} %get-tuple-element.5) | copy-start | bytes 6291460
  123.2 11.1 %copy-start.4 = (bf16[256,8192]{1,0:T(8,128)(2,1)}, bf16[256,8192]{1,0:T(8,128)(2,1)S(1)}, u32[]{:S(2)}) copy-start(bf16[256,8192]{1,0:T(8,128)(2,1)S(1)} %fusion) | copy-start | bytes 12582916
  134.4 2.0 copy-start.2
  137.7 4.5 %copy-start = (f32[8192,256]{1,0:T(8,128)}, f32[8192,256]{1,0:T(8,128)S(1)}, u32[]{:S(2)}) copy-start(f32[8192,256]{1,0:T(8,128)S(1)} %convolution_add_fusion) | copy-start | bytes 25165828
  142.2 29.5 %collective-permute-start.1 = (f32[4096,256]{1,0:T(8,128)}, f32[4096,256]{1,0:T(8,128)}, u32[]{:S(2)}, u32[]{:S(2)}) collective-permute-start(f32[4096,256]{1,0:T(8,128)} %slice_select_fusion), channel_id=1, source_target_pairs={{0,4},{4,0},{8,12},{12,8},{1,5},{5,1},{9,13},{13,9},{2,6},{6,2},{1... | collective-permute-start | bytes 12582920 | tf_op jit(solution)/shard_map/ppermute | solution.py:13
  142.2 4.7 %copy-start.3 = (bf16[256,8192]{1,0:T(8,128)(2,1)S(1)}, bf16[256,8192]{1,0:T(8,128)(2,1)}, u32[]{:S(2)}) copy-start(bf16[256,8192]{1,0:T(8,128)(2,1)} %copy-done.2) | copy-start | bytes 12582916
  142.2 4.8 %copy-start.7 = (bf16[4096,256]{1,0:T(8,128)(2,1)S(1)}, bf16[4096,256]{1,0:T(8,128)(2,1)}, u32[]{:S(2)}) copy-start(bf16[4096,256]{1,0:T(8,128)(2,1)} %get-tuple-element.5) | copy-start | bytes 6291460
  148.7 0.8 copy-start.5
  149.5 113.4 %all-reduce.8.cloned.1.call-start = ((), (), s32[]{:S(2)}) async-start(), calls=%async_computation.7 | async-start | bytes 524288 | tf_op jit(solution)/shard_map/psum | solution.py:73
  152.8 144.3 %all-reduce.6.cloned.1.call-start = ((), (), s32[]{:S(2)}) async-start(), calls=%async_computation.6 | async-start | bytes 262144 | tf_op jit(solution)/shard_map/psum | solution.py:72
  171.6 204.5 %reduce-scatter.3.cloned.1.call-start = ((), (), s32[]{:S(2)}) async-start(), calls=%async_computation.4 | async-start | bytes 5242880 | tf_op jit(solution)/shard_map/reduce_scatter | solution.py:67
Sparse Core Ops, SparseCore 0:
  9.6 48.6 all-gather.1
  67.5 50.0 all-reduce.3
  149.7 21.8 reduce-scatter.4
  175.8 87.1 all-reduce.7
  265.2 31.8 all-reduce.5
  299.3 76.7 reduce-scatter.2
where the time goes:
time: 385 us
  waiting for transfers between devices  311 us (81%)
  matrix products  30 us (8%)
  other arithmetic  21 us (5%)
  between operations  14.3 us (4%)
  blocking collectives  5.67 us (1%)
    reduce_scatter x1, waiting for transfers between devices, body(): lax.psum_scatter(mine + received, 'cuts', scatter_dimension=0, tiled=True)  77.4 us
    psum x1, waiting for transfers between devices, body(): core_total = lax.psum(acc_core, ('tile', 'cuts'))  76.4 us
    all_gather x1, waiting for transfers between devices, body(): own_block = lax.all_gather(factor, 'cuts', axis=0, tiled=True)  50.3 us
    psum x1, waiting for transfers between devices, from_root(): return lax.psum(block, axis)  50.2 us
    psum x1, waiting for transfers between devices, body(): window_total = lax.psum(window_part, 'tile')  32.5 us
    reduce_scatter x1, waiting for transfers between devices, body(): lax.psum_scatter(padded, 'cuts', scatter_dimension=0, tiled=True)  18.8 us
    dot_general x2, matrix products, body(): lax.dot_general(mapped, column_factor, (((1,), (1,)), ((), ())), preferre...  13.9 us
  transfers between devices with their start and end apart: 8, of which 7 were waited for; matrix products, arithmetic and copies ran while one was open for 6% of the time, Pallas kernels for 0%

commit v1 on v0

--- a/solution.py
+++ b/solution.py
@@ -69,7 +69,7 @@
         jnp.zeros((window_size, P_SIZE), jnp.float32), acc_window, band_index * rows_band, 0
     )
     window_part = lax.psum_scatter(padded, "cuts", scatter_dimension=0, tiled=True)
-    window_total = lax.psum(window_part, "tile")
+    window_total = jnp.sum(lax.all_gather(window_part, "tile"), axis=0)
     core_total = lax.psum(acc_core, ("tile", "cuts"))
     diag_total = lax.psum(diag_stack, "tile")
     return (-coef * grad_factor, -coef * window_total, -coef * core_total, -coef * diag_total)

time: 385 us -> 351 us (0.912)
  waiting for transfers between devices: 311 us -> 270 us
  blocking collectives: 5.67 us -> 13.8 us
    psum x1 -> x0, waiting for transfers between devices: 32.5 us -> none  [body(): window_total = lax.psum(window_part, 'tile')]
    reduce_scatter x1, waiting for transfers between devices: 77.4 us -> 69.4 us  [body(): lax.psum_scatter(mine + received, 'cuts', scatter_dimension=0, tiled=True)]
    all_gather x0 -> x1, blocking collectives: none -> 7.22 us  [body(): window_total = jnp.sum(lax.all_gather(window_part, 'tile'), axis=0)]
    psum x1, waiting for transfers between devices: 76.4 us -> 71.2 us  [body(): core_total = lax.psum(acc_core, ('tile', 'cuts'))]
    reduce_scatter x1, waiting for transfers between devices: 18.8 us -> 23.3 us  [body(): lax.psum_scatter(padded, 'cuts', scatter_dimension=0, tiled=True)]
  transfers between devices with their start and end apart: 8 -> 7, of which waited for: 7 -> 6; matrix products, arithmetic and copies ran while one was open for 6% -> 6% of each run, Pallas kernels for 0% -> 0%
where the time goes in v1:
time: 351 us
  waiting for transfers between devices  270 us (77%)
  matrix products  29.8 us (8%)
  other arithmetic  20.1 us (6%)
  between operations  14 us (4%)
  blocking collectives  13.8 us (4%)
    psum x1, waiting for transfers between devices, body(): core_total = lax.psum(acc_core, ('tile', 'cuts'))  71.2 us
    reduce_scatter x1, waiting for transfers between devices, body(): lax.psum_scatter(mine + received, 'cuts', scatter_dimension=0, tiled=True)  69.4 us
    all_gather x1, waiting for transfers between devices, body(): own_block = lax.all_gather(factor, 'cuts', axis=0, tiled=True)  50.3 us
    psum x1, waiting for transfers between devices, from_root(): return lax.psum(block, axis)  50.2 us
    reduce_scatter x1, waiting for transfers between devices, body(): lax.psum_scatter(padded, 'cuts', scatter_dimension=0, tiled=True)  23.3 us
    dot_general x2, matrix products, body(): lax.dot_general(mapped, column_factor, (((1,), (1,)), ((), ())), preferre...  13.7 us
    add x1, other arithmetic, body(): mine + received  7.43 us
    all_gather x1, blocking collectives, body(): window_total = jnp.sum(lax.all_gather(window_part, 'tile'), axis=0)  7.22 us
  transfers between devices with their start and end apart: 7, of which 6 were waited for; matrix products, arithmetic and copies ran while one was open for 6% of the time, Pallas kernels for 0%

profile of v1, /device:TPU:0, one launch (start us, length us, event | category | flops | bytes accessed | tf_op | source)
XLA Modules:
  0.0 351.0 jit_solution(10740695266044333695)
XLA Ops:
  7.2 0.0 all-gather.3.cloned.1.call-start
  7.2 0.7 all-gather.3.cloned.1.call-update
  7.9 0.0 all-reduce.3.cloned.1.call-start
  7.9 50.3 %all-gather.3.cloned.1.call-done = bf16[4096,256]{1,0:T(8,128)(2,1)} async-done(((bf16[1024,256]{1,0:T(8,128)(2,1)}), bf16[4096,256]{1,0:T(8,128)(2,1)}) %all-gather.3.cloned.1.call-update) | async-done | bytes 2097168 | tf_op jit(solution)/shard_map/all_gather | solution.py:28
  58.2 0.0 collective-permute-start
  58.2 4.5 %collective-permute-done = bf16[4096,256]{1,0:T(8,128)(2,1)} collective-permute-done((bf16[4096,256]{1,0:T(8,128)(2,1)}, bf16[4096,256]{1,0:T(8,128)(2,1)}, u32[]{:S(2)}, u32[]{:S(2)}) %collective-permute-start) | collective-permute-done | bytes 2097184 | tf_op jit(solution)/shard_map/ppermute | solution.py:13
  62.7 4.6 %broadcast_select_fusion.2 = (bf16[4096,256]{1,0:T(8,128)(2,1)S(1)}, bf16[4096,256]{1,0:T(8,128)(2,1)}, bf16[4096,256]{1,0:T(8,128)(2,1)}) fusion(bf16[4096,256]{1,0:T(8,128)(2,1)} %all-gather.3.cloned.1.call-done, bf16[4096,256]{1,0:T(8,128)(2,1)} %collective-permute-done, pred[]{:T(512)S(6)} %eq.6, pred[]{:T(512)S(6)} %eq.12), kind=kLoop, calls=%fused_computation.10 | loop fusion | flops 3145728 | bytes 10485762 | tf_op jit(solution)/shard_map/jit(_where)/select_n | solution.py:31
  67.4 0.0 all-reduce.3.cloned.1.call-update
  67.4 0.0 all-reduce.5.cloned.1.call-start
  67.5 50.2 %all-reduce.3.cloned.1.call-done = bf16[4096,256]{1,0:T(8,128)(2,1)} async-done(((bf16[4096,256]{1,0:T(8,128)(2,1)}), bf16[4096,256]{1,0:T(8,128)(2,1)}) %all-reduce.3.cloned.1.call-update) | async-done | bytes 2097168 | tf_op jit(solution)/shard_map/psum | solution.py:18
  117.6 1.3 convolution_convert_fusion.1
  118.9 4.3 %fusion = bf16[256,8192]{1,0:T(8,128)(2,1)S(1)} fusion(bf16[256,256]{1,0:T(8,128)(2,1)S(1)} %convolution_convert_fusion.1, bf16[2,1,256,8192]{3,2,1,0:T(8,128)(2,1)} %param.4, bf16[4096,256]{1,0:T(8,128)(2,1)} %get-tuple-element.5, bf16[4096,256]{1,0:T(8,128)(2,1)S(1)} %get-tuple-element.4), kind=kOutput, calls=%fused_computation.3 | convolution fusion | flops 1088421888 | bytes 12713984 | tf_op jit(solution)/shard_map/dot_general | solution.py:46
  123.2 1.5 convolution_convert_fusion
  124.7 9.4 %fusion.1 = bf16[256,8192]{1,0:T(8,128)(2,1)S(1)} fusion(bf16[256,256]{1,0:T(8,128)(2,1)S(1)} %convolution_convert_fusion, bf16[2,1,256,8192]{3,2,1,0:T(8,128)(2,1)} %param.4, bf16[4096,256]{1,0:T(8,128)(2,1)S(1)} %copy-done.6, bf16[4096,256]{1,0:T(8,128)(2,1)S(1)} %get-tuple-element.4), kind=kOutput, calls=%fused_computation.4 | convolution fusion | flops 1088421888 | bytes 12713984 | tf_op jit(solution)/shard_map/dot_general | solution.py:46
  134.2 1.3 fusion.43
  135.5 0.6 copy-done.2
  136.1 1.3 convolution_add_fusion
  137.5 2.8 slice_select_fusion
  140.3 1.6 copy-done
  142.0 0.0 collective-permute-start.1
  142.0 4.2 %fusion.41 = f32[256,256]{1,0:T(8,128)S(1)} fusion(bf16[256,8192]{1,0:T(8,128)(2,1)} %copy-done.4, bf16[4096,256]{1,0:T(8,128)(2,1)} %get-tuple-element.5, bf16[4096,256]{1,0:T(8,128)(2,1)S(1)} %get-tuple-element.4), kind=kOutput, calls=%fused_computation.61 | convolution fusion | flops 1082130432 | bytes 8650752 | tf_op jit(solution)/shard_map/dot_general | solution.py:53
  146.2 1.2 fusion.24
  147.5 1.2 fusion.40
  148.7 1.9 multiply_add_fusion
  150.7 0.0 all-reduce.5.cloned.1.call-update
  150.7 0.2 reduce-scatter.5.cloned.1.call-start
  150.9 0.5 fusion.7
  151.4 0.5 fusion.2
  151.9 0.0 copy-start.5
  152.0 0.8 copy-done.5
  152.7 0.0 reduce-scatter.5.cloned.1.call-update
  152.8 0.0 reduce-scatter.3.cloned.1.call-start
  152.8 0.0 collective-permute-done.1
  152.8 7.4 %select_add_fusion = f32[4096,256]{1,0:T(8,128)} fusion(f32[4096,256]{1,0:T(8,128)} %collective-permute-done.1, f32[8192,256]{1,0:T(8,128)} %copy-done, pred[]{:T(512)S(6)} %eq.6), kind=kLoop, calls=%fused_computation.6 | loop fusion | flops 2097152 | bytes 16777216 | tf_op jit(solution)/shard_map/add | solution.py:67
  160.3 0.0 reduce-scatter.3.cloned.1.call-update
  160.3 0.3 fusion.20
  160.6 0.3 fusion.5
  160.8 0.3 fusion.17
  161.1 0.3 fusion.3
  161.5 6.6 %psum.23 = f32[2,256]{1,0:T(2,128)S(1)} all-reduce(f32[2,256]{1,0:T(2,128)S(1)} %pad_maximum_fusion.1), channel_id=1, replica_groups=mesh['groups'=2,'tile'=4,'cuts'=4] {'tile'}, use_global_device_ids=true, to_apply=%region_5.6 | all-reduce | flops 512 | bytes 4096 | tf_op jit(solution)/shard_map/psum | solution.py:74
  168.1 0.6 broadcast_multiply_fusion.3
  168.6 71.2 %all-reduce.5.cloned.1.call-done = f32[256,256]{1,0:T(8,128)} async-done(((f32[256,256]{1,0:T(8,128)}), f32[256,256]{1,0:T(8,128)}) %all-reduce.5.cloned.1.call-update) | async-done | bytes 262160 | tf_op jit(solution)/shard_map/psum | solution.py:73
  239.9 1.7 broadcast_multiply_fusion.1
  241.6 23.3 %reduce-scatter.5.cloned.1.call-done = f32[128,256]{1,0:T(8,128)} async-done(((f32[512,256]{1,0:T(8,128)}), f32[128,256]{1,0:T(8,128)}) %reduce-scatter.5.cloned.1.call-update) | async-done | bytes 131088 | tf_op jit(solution)/shard_map/reduce_scatter | solution.py:71
  264.9 7.2 %all-gather = f32[512,256]{1,0:T(8,128)S(1)} all-gather(f32[128,256]{1,0:T(8,128)} %reduce-scatter.5.cloned.1.call-done), channel_id=2, replica_groups=mesh['groups'=2,'tile'=4,'cuts'=4] {'tile'}, dimensions={0}, use_global_device_ids=true | all-gather | bytes 655360 | tf_op jit(solution)/shard_map/all_gather | solution.py:72
  272.2 0.7 broadcast_multiply_fusion.2
  272.8 69.4 %reduce-scatter.3.cloned.1.call-done = f32[1024,256]{1,0:T(8,128)} async-done(((f32[4096,256]{1,0:T(8,128)}), f32[1024,256]{1,0:T(8,128)}) %reduce-scatter.3.cloned.1.call-update) | async-done | bytes 1048592 | tf_op jit(solution)/shard_map/reduce_scatter | solution.py:67
  342.3 2.3 broadcast_multiply_fusion
  (20 shorter events, 0.1 us)
Async XLA Ops:
  7.2 51.1 %all-gather.3.cloned.1.call-start = ((), (), s32[]{:S(2)}) async-start(), calls=%async_computation.2 | async-start | bytes 2621440 | tf_op jit(solution)/shard_map/all_gather | solution.py:28
  7.9 109.7 %all-reduce.3.cloned.1.call-start = ((), (), s32[]{:S(2)}) async-start(), calls=%async_computation.3 | async-start | bytes 4194304 | tf_op jit(solution)/shard_map/psum | solution.py:18
  58.2 4.5 %collective-permute-start = (bf16[4096,256]{1,0:T(8,128)(2,1)}, bf16[4096,256]{1,0:T(8,128)(2,1)}, u32[]{:S(2)}, u32[]{:S(2)}) collective-permute-start(bf16[4096,256]{1,0:T(8,128)(2,1)} %all-gather.3.cloned.1.call-done), channel_id=1, source_target_pairs={{0,4},{4,0},{8,12},{12,8},{1,5},{5,1},{9,13},{13,9},{2,6},{6,2},{1... | collective-permute-start | bytes 6291464 | tf_op jit(solution)/shard_map/ppermute | solution.py:13
  58.2 9.2 %copy-start.8 = (f32[2,256]{1,0:T(2,128)S(1)}, f32[2,256]{1,0:T(2,128)}, u32[]{:S(2)}) copy-start(f32[2,256]{1,0:T(2,128)} %param.6) | copy-start | bytes 6148
  58.2 59.4 %copy-start.1 = (f32[256,256]{1,0:T(8,128)S(1)}, f32[256,256]{1,0:T(8,128)}, u32[]{:S(2)}) copy-start(f32[256,256]{1,0:T(8,128)} %param.7) | copy-start | bytes 786436
  67.4 172.5 %all-reduce.5.cloned.1.call-start = ((), (), s32[]{:S(2)}) async-start(), calls=%async_computation.6 | async-start | bytes 524288 | tf_op jit(solution)/shard_map/psum | solution.py:73
  118.9 5.8 %copy-start.6 = (bf16[4096,256]{1,0:T(8,128)(2,1)S(1)}, bf16[4096,256]{1,0:T(8,128)(2,1)}, u32[]{:S(2)}) copy-start(bf16[4096,256]{1,0:T(8,128)(2,1)} %get-tuple-element.5) | copy-start | bytes 6291460
  123.2 10.9 %copy-start.4 = (bf16[256,8192]{1,0:T(8,128)(2,1)}, bf16[256,8192]{1,0:T(8,128)(2,1)S(1)}, u32[]{:S(2)}) copy-start(bf16[256,8192]{1,0:T(8,128)(2,1)S(1)} %fusion) | copy-start | bytes 12582916
  134.2 2.0 copy-start.2
  137.5 4.5 %copy-start = (f32[8192,256]{1,0:T(8,128)}, f32[8192,256]{1,0:T(8,128)S(1)}, u32[]{:S(2)}) copy-start(f32[8192,256]{1,0:T(8,128)S(1)} %convolution_add_fusion) | copy-start | bytes 25165828
  142.0 10.9 %collective-permute-start.1 = (f32[4096,256]{1,0:T(8,128)}, f32[4096,256]{1,0:T(8,128)}, u32[]{:S(2)}, u32[]{:S(2)}) collective-permute-start(f32[4096,256]{1,0:T(8,128)} %slice_select_fusion), channel_id=1, source_target_pairs={{0,4},{4,0},{8,12},{12,8},{1,5},{5,1},{9,13},{13,9},{2,6},{6,2},{1... | collective-permute-start | bytes 12582920 | tf_op jit(solution)/shard_map/ppermute | solution.py:13
  142.0 5.5 %copy-start.3 = (bf16[256,8192]{1,0:T(8,128)(2,1)S(1)}, bf16[256,8192]{1,0:T(8,128)(2,1)}, u32[]{:S(2)}) copy-start(bf16[256,8192]{1,0:T(8,128)(2,1)} %copy-done.2) | copy-start | bytes 12582916
  142.0 5.5 %copy-start.7 = (bf16[4096,256]{1,0:T(8,128)(2,1)S(1)}, bf16[4096,256]{1,0:T(8,128)(2,1)}, u32[]{:S(2)}) copy-start(bf16[4096,256]{1,0:T(8,128)(2,1)} %get-tuple-element.5) | copy-start | bytes 6291460
  150.7 114.2 %reduce-scatter.5.cloned.1.call-start = ((), (), s32[]{:S(2)}) async-start(), calls=%async_computation.5 | async-start | bytes 655360 | tf_op jit(solution)/shard_map/reduce_scatter | solution.py:71
  151.9 0.8 copy-start.5
  152.8 189.5 %reduce-scatter.3.cloned.1.call-start = ((), (), s32[]{:S(2)}) async-start(), calls=%async_computation.4 | async-start | bytes 5242880 | tf_op jit(solution)/shard_map/reduce_scatter | solution.py:67
Sparse Core Ops, SparseCore 0:
  9.6 48.6 all-gather.2
  67.5 50.0 all-reduce.2
  150.8 89.0 all-reduce.4
  242.7 22.1 reduce-scatter.4
  267.1 75.0 reduce-scatter.2
